TPU v7x, 32 devices: a whole 2x2x4 slice. The times are simulated.
32 devices in a mesh: blk: 16 (over z, y, x), beamk: 2 (over core).
Axes of the slice: x: 2, y: 2, z: 4, core: 2. Of those that a mesh axis runs over, the one named last changes fastest.
Arguments:
- sky: bfloat16 [32, 3072, 384], P('blk', 'beamk'), may hold values from -6 to 6
- beam: float32 [40, 2, 3072], P('beamk'), may hold values from -6 to 6
- wigner: bfloat16 [32, 40, 16, 3072], P('blk', 'beamk'), may hold values from -0.109375 to 0.109375
- m_list: int32 [32], P('blk'), may hold values from 0 to 3071, as said below
Outputs:
- cycle_coeffs: bfloat16 [16, 32, 40, 384], P('blk', None, 'beamk')
Inputs may be any that keep to these rules, and one draw needn't show every extreme that they name: `m_list`: entries 2i and 2i+1 hold m and 3071-m for some m below 1536; all entries are distinct, and some slot holds 0.
All inputs are finite; a program needn't handle non-finite values.
Results may differ from a plain program's by a relative error of at most 0.0049.
Values may be sent and summed in bfloat16 or wider, within the bound.
No kernel may reach another device: no remote copies, remote signals or barrier semaphores. Data moves between devices by JAX's collectives and lax.ppermute only.
A program may use at most 64 MiB of HBM per device.

v0:
```python
import jax
import jax.numpy as jnp
from jax import lax
from jax.sharding import PartitionSpec as P

KB = 40


def slot_term(sky_rows, wigner_rows, lowest_slot, degrees, beam_re, beam_im):
    sims = sky_rows.shape[1] // 2
    sky_re = sky_rows[:, :sims].astype(jnp.float32)
    sky_im = sky_rows[:, sims:].astype(jnp.float32)
    prod_re = sky_re[None] * beam_re[:, :, None] - sky_im[None] * beam_im[:, :, None]
    prod_im = sky_re[None] * beam_im[:, :, None] + sky_im[None] * beam_re[:, :, None]
    product = jnp.concatenate([prod_re, prod_im], axis=-1)
    inside = degrees[None, :] >= lowest_slot[:, None]
    product = jnp.where(inside[:, :, None], product, jnp.zeros_like(product)).astype(jnp.bfloat16)
    return jnp.einsum("krl,kls->rks", wigner_rows, product, preferred_element_type=jnp.float32)


def local(sky, beam, wigner, m_list):
    slot_count = sky.shape[0]
    k_local = beam.shape[0]
    cycle_count = wigner.shape[2]
    columns = sky.shape[2]
    k_offset = KB // 2
    k_values = lax.axis_index("beamk") * k_local + jnp.arange(k_local, dtype=jnp.int32) - k_offset
    lowest = jnp.maximum(m_list[:, None], jnp.abs(k_values)[None, :])
    beam_re_all = beam[:, 0, :]
    beam_im_all = beam[:, 1, :]
    initial = jnp.zeros((cycle_count, slot_count, k_local, columns), jnp.float32)
    running = initial
    sky_piece = lax.all_gather(sky, "beamk", axis=1, tiled=True)
    first_row = jnp.int32(0)
    row_count = sky_piece.shape[1]
    for offset in range(0, row_count, 512):
        span_rows = min(512, row_count - offset)
        row_start = first_row + offset
        degrees = row_start + jnp.arange(span_rows, dtype=jnp.int32)
        beam_re = lax.dynamic_slice_in_dim(beam_re_all, row_start, span_rows, 1)
        beam_im = lax.dynamic_slice_in_dim(beam_im_all, row_start, span_rows, 1)
        wigner_rows = lax.dynamic_slice_in_dim(wigner, row_start, span_rows, 3)
        sky_block = sky_piece[:, offset : offset + span_rows, :]
        updated = []
        for slot in range(slot_count):

            def with_term(current, slot=slot):
                return current + slot_term(
                    sky_block[slot], wigner_rows[slot], lowest[slot], degrees, beam_re, beam_im
                )

            current = running[:, slot]
            updated.append(with_term(current))
        running = jnp.stack(updated, axis=1)
    return lax.all_to_all(
        running.astype(jnp.bfloat16), "blk", split_axis=0, concat_axis=1, tiled=True
    )


def solution(mesh):
    in_specs = (
        P("blk", "beamk", None),
        P("beamk", None, None),
        P("blk", "beamk", None, None),
        P("blk"),
    )
    out_specs = P("blk", None, "beamk", None)
    return jax.shard_map(local, mesh=mesh, in_specs=in_specs, out_specs=out_specs, check_vma=False)
```

profile of v0, /device:TPU:0, one launch (start us, length us, event | category | flops | bytes accessed | tf_op | source)
XLA Modules:
  0.0 179.2 jit_solution(11304295205343752274)
XLA Ops:
  6.5 0.0 all-gather.2.cloned.1.call-start
  6.5 0.7 all-gather.2.cloned.1.call-update
  7.3 0.7 broadcast_maximum_fusion
  8.0 0.8 broadcast_compare_fusion.9
  8.8 1.6 fusion.138
  10.4 0.1 copy_bitcast_fusion
  10.6 15.5 %all-gather.2.cloned.1.call-done = bf16[2,3072,384]{2,1,0:T(8,128)(2,1)} async-done(((bf16[2,1536,384]{2,1,0:T(8,128)(2,1)}), bf16[2,3072,384]{2,1,0:T(8,128)(2,1)}) %all-gather.2.cloned.1.call-update) | async-done | bytes 4718608 | tf_op jit(solution)/shard_map/all_gather | solution.py:33
  26.1 2.8 %slice_bitcast_fusion.6 = (bf16[512,384]{1,0:T(8,128)(2,1)S(1)}, bf16[512,384]{1,0:T(8,128)(2,1)S(1)}, bf16[512,384]{1,0:T(8,128)(2,1)S(1)}, bf16[512,384]{1,0:T...) fusion(bf16[2,3072,384]{2,1,0:T(8,128)(2,1)} %all-gather.2.clon, ...), kind=kLoop, calls=%fused_computation.93 | loop fusion | bytes 9437184 | tf_op jit(solution)/shard_map/squeeze | solution.py:49
  28.9 0.3 slice_convert_fusion.13
  29.2 0.3 slice_convert_fusion.1
  29.4 0.3 slice_convert_fusion.5
  29.7 0.3 slice_convert_fusion.9
  29.9 0.3 slice_convert_fusion.17
  30.2 0.2 slice_convert_fusion.21
  30.5 0.0 copy-start.1
  30.5 5.7 %multiply_subtract_fusion.10 = (bf16[20,512,192]{2,1,0:T(8,128)(2,1)S(1)}, bf16[20,512,192]{2,1,0:T(8,128)(2,1)S(1)}, bf16[20,512,192]{2,1,0:T(8,128)(2,1)S(1)}, bf16[20,512,192]{2,1,0:T(8,128)(2,1)S(1)}) fusion(f32[20,512]{1,0:T(8,128)S(1)} %get-tuple-element.77, f32[512,192]{1,0:T(8,128)S(1)} %get-tuple-element.54, f32[20,512]{1,0:T(8,128)S(1)} %get-tuple-element.71, ...), kind=kLoop, calls=%fused_computation.45 | loop fusion | flops 31457280 | bytes 17383424 | tf_op jit(solution)/shard_map/sub | solution.py:13
  36.2 0.0 copy-done.1
  36.2 7.4 %fusion.32 = f32[20,384,16]{1,2,0:T(8,128)S(1)} fusion(bf16[20,512,192]{2,1,0:T(8,128)(2,1)S(1)} %get-tuple-element.28, bf16[20,512,192]{2,1,0:T(8,128)(2,1)S(1)} %get-tuple-element.27, pred[20,512]{1,0:T(8,128)(4,1)S(1)} %get-tuple-element.99, bf16[2,20,16,3072]{3,2,1,0:T(8,128)(2,1)S(1)} %copy-done.1), kind=kOutput, calls=%fused_computation.58 | convolution fusion | flops 145489920 | bytes 11317248 | tf_op jit(solution)/shard_map/krl,kls->rks/dot_general | solution.py:18
  43.6 7.3 %fusion.20 = f32[20,384,16]{1,2,0:T(8,128)S(1)} fusion(bf16[20,512,192]{2,1,0:T(8,128)(2,1)S(1)} %get-tuple-element.89, bf16[20,512,192]{2,1,0:T(8,128)(2,1)S(1)} %get-tuple-element.90, pred[20,512]{1,0:T(8,128)(4,1)S(1)} %get-tuple-element.100, bf16[2,20,16,3072]{3,2,1,0:T(8,128)(2,1)S(1)} %copy-done.1), kind=kOutput, calls=%fused_computation.52 | convolution fusion | flops 145489920 | bytes 11317248 | tf_op jit(solution)/shard_map/krl,kls->rks/dot_general | solution.py:18
  50.9 5.7 %multiply_subtract_fusion.11 = (bf16[20,512,192]{2,1,0:T(8,128)(2,1)S(1)}, bf16[20,512,192]{2,1,0:T(8,128)(2,1)S(1)}, bf16[20,512,192]{2,1,0:T(8,128)(2,1)S(1)}, bf16[20,512,192]{2,1,0:T(8,128)(2,1)S(1)}) fusion(f32[20,512]{1,0:T(8,128)S(1)} %get-tuple-element.78, f32[512,192]{1,0:T(8,128)S(1)} %get-tuple-element.125, f32[20,512]{1,0:T(8,128)S(1)} %get-tuple-element.72, ...), kind=kLoop, calls=%fused_computation.47 | loop fusion | flops 31457280 | bytes 17383424 | tf_op jit(solution)/shard_map/sub | solution.py:13
  56.6 7.4 %fusion.63 = f32[20,384,16]{1,2,0:T(8,128)S(1)} fusion(f32[20,384,16]{1,2,0:T(8,128)S(1)} %fusion.20, bf16[20,512,192]{2,1,0:T(8,128)(2,1)S(1)} %get-tuple-element.87, bf16[20,512,192]{2,1,0:T(8,128)(2,1)S(1)} %get-tuple-element.88, pred[20,512]{1,0:T(8,128)(4,1)S(1)} %get-tuple-element.111, bf16[2,20,16,3072]{3,2,1,0:T(8,128)(2,1)S(1)} %copy-done.1), kind=kOutput, calls=%fused_computation.77 | convolution fusion | flops 145612800 | bytes 11808768 | tf_op jit(solution)/shard_map/krl,kls->rks/dot_general | solution.py:18
  64.0 7.4 %fusion.48 = f32[20,384,16]{1,2,0:T(8,128)S(1)} fusion(f32[20,384,16]{1,2,0:T(8,128)S(1)} %fusion.32, bf16[20,512,192]{2,1,0:T(8,128)(2,1)S(1)} %get-tuple-element.26, bf16[20,512,192]{2,1,0:T(8,128)(2,1)S(1)} %get-tuple-element.25, pred[20,512]{1,0:T(8,128)(4,1)S(1)} %get-tuple-element.112, bf16[2,20,16,3072]{3,2,1,0:T(8,128)(2,1)S(1)} %copy-done.1), kind=kOutput, calls=%fused_computation.72 | convolution fusion | flops 145612800 | bytes 11808768 | tf_op jit(solution)/shard_map/krl,kls->rks/dot_general | solution.py:18
  71.4 5.7 %multiply_subtract_fusion.9 = (bf16[20,512,192]{2,1,0:T(8,128)(2,1)S(1)}, bf16[20,512,192]{2,1,0:T(8,128)(2,1)S(1)}, bf16[20,512,192]{2,1,0:T(8,128)(2,1)S(1)}, bf16[20,512,192]{2,1,0:T(8,128)(2,1)S(1)}) fusion(f32[20,512]{1,0:T(8,128)S(1)} %get-tuple-element.76, f32[512,192]{1,0:T(8,128)S(1)} %get-tuple-element.123, f32[20,512]{1,0:T(8,128)S(1)} %get-tuple-element.70, ...), kind=kLoop, calls=%fused_computation.43 | loop fusion | flops 31457280 | bytes 17383424 | tf_op jit(solution)/shard_map/sub | solution.py:13
  77.1 7.4 %fusion.66 = f32[20,384,16]{1,2,0:T(8,128)S(1)} fusion(f32[20,384,16]{1,2,0:T(8,128)S(1)} %fusion.63, bf16[20,512,192]{2,1,0:T(8,128)(2,1)S(1)} %get-tuple-element.85, bf16[20,512,192]{2,1,0:T(8,128)(2,1)S(1)} %get-tuple-element.86, pred[20,512]{1,0:T(8,128)(4,1)S(1)} %get-tuple-element.107, bf16[2,20,16,3072]{3,2,1,0:T(8,128)(2,1)S(1)} %copy-done.1), kind=kOutput, calls=%fused_computation.78 | convolution fusion | flops 145612800 | bytes 11808768 | tf_op jit(solution)/shard_map/krl,kls->rks/dot_general | solution.py:18
  84.5 5.7 %multiply_subtract_fusion.8 = (bf16[20,512,192]{2,1,0:T(8,128)(2,1)S(1)}, bf16[20,512,192]{2,1,0:T(8,128)(2,1)S(1)}, bf16[20,512,192]{2,1,0:T(8,128)(2,1)S(1)}, bf16[20,512,192]{2,1,0:T(8,128)(2,1)S(1)}) fusion(f32[20,512]{1,0:T(8,128)S(1)} %get-tuple-element.75, f32[512,192]{1,0:T(8,128)S(1)} %get-tuple-element.48, f32[20,512]{1,0:T(8,128)S(1)} %get-tuple-element.69, ...), kind=kLoop, calls=%fused_computation.41 | loop fusion | flops 31457280 | bytes 17383424 | tf_op jit(solution)/shard_map/sub | solution.py:13
  90.2 7.1 %fusion.69 = f32[20,384,16]{1,2,0:T(8,128)S(1)} fusion(f32[20,384,16]{1,2,0:T(8,128)S(1)} %fusion.66, bf16[20,512,192]{2,1,0:T(8,128)(2,1)S(1)} %get-tuple-element.83, bf16[20,512,192]{2,1,0:T(8,128)(2,1)S(1)} %get-tuple-element.84, pred[20,512]{1,0:T(8,128)(4,1)S(1)} %get-tuple-element.105, bf16[2,20,16,3072]{3,2,1,0:T(8,128)(2,1)} %param.6), kind=kOutput, calls=%fused_computation.79 | convolution fusion | flops 145612800 | bytes 9185280 | tf_op jit(solution)/shard_map/krl,kls->rks/dot_general | solution.py:18
  97.4 7.1 %fusion.51 = f32[20,384,16]{1,2,0:T(8,128)S(1)} fusion(f32[20,384,16]{1,2,0:T(8,128)S(1)} %fusion.48, bf16[20,512,192]{2,1,0:T(8,128)(2,1)S(1)} %get-tuple-element.24, bf16[20,512,192]{2,1,0:T(8,128)(2,1)S(1)} %get-tuple-element.23, pred[20,512]{1,0:T(8,128)(4,1)S(1)} %get-tuple-element.108, bf16[2,20,16,3072]{3,2,1,0:T(8,128)(2,1)} %param.6), kind=kOutput, calls=%fused_computation.73 | convolution fusion | flops 145612800 | bytes 9185280 | tf_op jit(solution)/shard_map/krl,kls->rks/dot_general | solution.py:18
  104.5 7.1 %fusion.54 = f32[20,384,16]{1,2,0:T(8,128)S(1)} fusion(f32[20,384,16]{1,2,0:T(8,128)S(1)} %fusion.51, bf16[20,512,192]{2,1,0:T(8,128)(2,1)S(1)} %get-tuple-element.22, bf16[20,512,192]{2,1,0:T(8,128)(2,1)S(1)} %get-tuple-element.21, pred[20,512]{1,0:T(8,128)(4,1)S(1)} %get-tuple-element.106, bf16[2,20,16,3072]{3,2,1,0:T(8,128)(2,1)} %param.6), kind=kOutput, calls=%fused_computation.74 | convolution fusion | flops 145612800 | bytes 9185280 | tf_op jit(solution)/shard_map/krl,kls->rks/dot_general | solution.py:18
  111.6 0.0 copy-start.2
  111.6 5.7 %multiply_subtract_fusion.7 = (bf16[20,512,192]{2,1,0:T(8,128)(2,1)S(1)}, bf16[20,512,192]{2,1,0:T(8,128)(2,1)S(1)}, bf16[20,512,192]{2,1,0:T(8,128)(2,1)S(1)}, bf16[20,512,192]{2,1,0:T(8,128)(2,1)S(1)}) fusion(f32[20,512]{1,0:T(8,128)S(1)} %get-tuple-element.74, f32[512,192]{1,0:T(8,128)S(1)} %get-tuple-element.121, f32[20,512]{1,0:T(8,128)S(1)} %get-tuple-element.68, ...), kind=kLoop, calls=%fused_computation.39 | loop fusion | flops 31457280 | bytes 17383424 | tf_op jit(solution)/shard_map/sub | solution.py:13
  117.4 0.0 copy-done.2
  117.4 7.4 %fusion.72 = f32[20,384,16]{1,2,0:T(8,128)S(1)} fusion(f32[20,384,16]{1,2,0:T(8,128)S(1)} %fusion.69, bf16[20,512,192]{2,1,0:T(8,128)(2,1)S(1)} %get-tuple-element.81, bf16[20,512,192]{2,1,0:T(8,128)(2,1)S(1)} %get-tuple-element.82, pred[20,512]{1,0:T(8,128)(4,1)S(1)} %get-tuple-element.103, bf16[2,20,16,3072]{3,2,1,0:T(8,128)(2,1)S(1)} %copy-done.2), kind=kOutput, calls=%fused_computation.80 | convolution fusion | flops 145612800 | bytes 11808768 | tf_op jit(solution)/shard_map/krl,kls->rks/dot_general | solution.py:18
  124.8 5.7 %multiply_subtract_fusion.6 = (bf16[20,512,192]{2,1,0:T(8,128)(2,1)S(1)}, bf16[20,512,192]{2,1,0:T(8,128)(2,1)S(1)}, bf16[20,512,192]{2,1,0:T(8,128)(2,1)S(1)}, bf16[20,512,192]{2,1,0:T(8,128)(2,1)S(1)}) fusion(f32[20,512]{1,0:T(8,128)S(1)} %get-tuple-element.73, f32[512,192]{1,0:T(8,128)S(1)} %get-tuple-element.44, f32[20,512]{1,0:T(8,128)S(1)} %get-tuple-element.67, ...), kind=kLoop, calls=%fused_computation.37 | loop fusion | flops 31457280 | bytes 17383424 | tf_op jit(solution)/shard_map/sub | solution.py:13
  130.5 5.6 %fusion.87 = bf16[16,1,20,384]{3,0,2,1:T(8,128)(2,1)S(1)} fusion(f32[20,384,16]{1,2,0:T(8,128)S(1)} %fusion.72, bf16[20,512,192]{2,1,0:T(8,128)(2,1)S(1)} %get-tuple-element.79, bf16[20,512,192]{2,1,0:T(8,128)(2,1)S(1)} %get-tuple-element.80, pred[20,512]{1,0:T(8,128)(4,1)S(1)} %get-tuple-element.101, bf16[2,20,16,3072]{3,2,1,0:T(8,128)(2,1)S(1)} %copy-done.2), kind=kOutput, calls=%fused_computation.85 | convolution fusion | flops 145735680 | bytes 11563008 | tf_op jit(solution)/shard_map/krl,kls->rks/dot_general | solution.py:18
  136.1 0.0 copy-start
  136.1 7.4 %fusion.57 = f32[20,384,16]{1,2,0:T(8,128)S(1)} fusion(f32[20,384,16]{1,2,0:T(8,128)S(1)} %fusion.54, bf16[20,512,192]{2,1,0:T(8,128)(2,1)S(1)} %get-tuple-element.20, bf16[20,512,192]{2,1,0:T(8,128)(2,1)S(1)} %get-tuple-element.19, pred[20,512]{1,0:T(8,128)(4,1)S(1)} %get-tuple-element.104, bf16[2,20,16,3072]{3,2,1,0:T(8,128)(2,1)S(1)} %copy-done.2), kind=kOutput, calls=%fused_computation.75 | convolution fusion | flops 145612800 | bytes 11808768 | tf_op jit(solution)/shard_map/krl,kls->rks/dot_general | solution.py:18
  143.4 0.0 copy-done
  143.4 5.6 %fusion.84 = bf16[16,1,20,384]{3,0,2,1:T(8,128)(2,1)S(1)} fusion(f32[20,384,16]{1,2,0:T(8,128)S(1)} %fusion.57, bf16[20,512,192]{2,1,0:T(8,128)(2,1)S(1)} %get-tuple-element.18, bf16[20,512,192]{2,1,0:T(8,128)(2,1)S(1)} %get-tuple-element.17, pred[20,512]{1,0:T(8,128)(4,1)S(1)} %copy-done, bf16[2,20,16,3072]{3,2,1,0:T(8,128)(2,1)S(1)} %copy-done.2), kind=kOutput, calls=%fused_computation.84 | convolution fusion | flops 145735680 | bytes 11563008 | tf_op jit(solution)/shard_map/krl,kls->rks/dot_general | solution.py:18
  149.0 0.1 pad_maximum_fusion
  149.1 0.5 copy.14
  149.6 21.5 %all_to_all.12 = bf16[16,2,20,384]{3,1,2,0:T(2,128)(2,1)S(1)} all-to-all(bf16[16,2,20,384]{3,1,2,0:T(2,128)(2,1)S(1)} %copy.14), channel_id=1, replica_groups=mesh['blk'=16,'beamk'=2] {'blk'}, dimensions={0} | all-to-all | bytes 983040 | tf_op jit(solution)/shard_map/all_to_all | solution.py:55
  171.1 0.3 copy.15
  171.4 1.0 all_to_all.10
  (7 shorter events, 0.1 us)
Async XLA Ops:
  6.5 19.5 %all-gather.2.cloned.1.call-start = ((), (), s32[]{:S(2)}) async-start(), calls=%async_computation.1 | async-start | bytes 7077888 | tf_op jit(solution)/shard_map/all_gather | solution.py:33
  30.5 5.7 %copy-start.1 = (bf16[2,20,16,3072]{3,2,1,0:T(8,128)(2,1)S(1)}, bf16[2,20,16,3072]{3,2,1,0:T(8,128)(2,1)}, u32[]{:S(2)}) copy-start(bf16[2,20,16,3072]{3,2,1,0:T(8,128)(2,1)} %param.6) | copy-start | bytes 11796484
  111.6 5.7 %copy-start.2 = (bf16[2,20,16,3072]{3,2,1,0:T(8,128)(2,1)S(1)}, bf16[2,20,16,3072]{3,2,1,0:T(8,128)(2,1)}, u32[]{:S(2)}) copy-start(bf16[2,20,16,3072]{3,2,1,0:T(8,128)(2,1)} %param.6) | copy-start | bytes 11796484
  136.1 7.4 %copy-start = (pred[20,512]{1,0:T(8,128)(4,1)S(1)}, pred[20,512]{1,0:T(8,128)(4,1)}, u32[]{:S(2)}) copy-start(pred[20,512]{1,0:T(8,128)(4,1)} %get-tuple-element.102) | copy-start | bytes 30724
Sparse Core Ops, SparseCore 0:
  8.9 17.1 all-gather.1
where the time goes:
time: 181 us; the launch traced here: 179 us
  matrix products  84.2 us (47%)
  other arithmetic  37.4 us (21%)
  blocking collectives  21.5 us (12%)
  waiting for transfers between devices  16.2 us (9%)
  between operations  13.6 us (8%)
  local copies, waits for them, and re-layouts  6.4 us (4%)
    dot_general x12, matrix products, slot_term(): jnp.einsum('krl,kls->rks', wigner_rows, product, preferred_element_type=j...  84.2 us
    sub x6, other arithmetic, slot_term(): sky_re[None] * beam_re[:, :, None] - sky_im[None] * beam_im[:, :, None]  34.3 us
    all_to_all x1, blocking collectives, local(): lax.all_to_all(running.astype(jnp.bfloat16), 'blk', split_axis=0, concat_...  21.5 us
    all_gather x1, waiting for transfers between devices, local(): sky_piece = lax.all_gather(sky, 'beamk', axis=1, tiled=True)  15.5 us
  transfers between devices with their start and end apart: 1, of which 1 were waited for; matrix products, arithmetic and copies ran while one was open for 2% of the time, Pallas kernels for 0%

commit v1 on v0

v1 whole, which is shorter than its diff:
```python
import functools

import jax
import jax.numpy as jnp
from jax import lax
from jax.experimental import pallas as pl
from jax.experimental.pallas import tpu as pltpu
from jax.sharding import PartitionSpec as P

KB = 40


def tile_of(rows):
    return max(t for t in range(128, min(rows, 512) + 1, 128) if rows % t == 0)


def combine(acc, width):
    re_rows = acc.shape[0] // 2
    first = acc[:re_rows]
    second = acc[re_rows:]
    half = width // 2
    swapped = pltpu.roll(second, half, 1)
    column = lax.broadcasted_iota(jnp.int32, swapped.shape, 1)
    return first + jnp.where(column < half, -swapped, swapped)


def kernel(tile, tiles, initial, final, meta, *refs):
    if initial:
        sky_ref, wigner_ref, beam_ref, out_ref, factor, acc = refs[:6]
        rest = refs[6:]
    else:
        sky_ref, wigner_ref, beam_ref, before_ref, out_ref, factor, acc = refs[:7]
        rest = refs[7:]
    slot, step = pl.program_id(0), pl.program_id(1)
    slots = pl.num_programs(0)
    k_local, cycles = wigner_ref.shape[1], wigner_ref.shape[2]
    rows = k_local * cycles
    m_value = meta[2 + slot]
    first_tile = meta[4 + slot]

    @pl.when(step == 0)
    def _():
        acc[...] = jnp.zeros_like(acc)

    @pl.when(step >= first_tile)
    def _():
        degrees = meta[0] + step * tile + lax.broadcasted_iota(jnp.int32, (1, tile), 1)
        for k in range(k_local):
            lowest = jnp.maximum(m_value, jnp.abs(meta[1] + k))
            inside = degrees >= lowest
            w = wigner_ref[0, k].astype(jnp.float32)
            beam_re = jnp.where(inside, beam_ref[k, 0:1, :], 0.0)
            beam_im = jnp.where(inside, beam_ref[k, 1:2, :], 0.0)
            factor[k * cycles : (k + 1) * cycles, :] = (w * beam_re).astype(jnp.bfloat16)
            factor[rows + k * cycles : rows + (k + 1) * cycles, :] = (w * beam_im).astype(jnp.bfloat16)
        acc[...] += jnp.dot(factor[...], sky_ref[0], preferred_element_type=jnp.float32)

    @pl.when(step == tiles - 1)
    def _():
        total = combine(acc[...], acc.shape[1])
        if not initial:
            total = total + before_ref[0]
        if final:
            turned = rest[0]
            for lanes in range(turned.shape[0]):
                span = slice(lanes * 128, (lanes + 1) * 128)
                for k in range(k_local):
                    turned[lanes, pl.ds(k, cycles, stride=k_local), :] = total[k * cycles : (k + 1) * cycles, span]
                out_ref[0, :, span] = turned[lanes].astype(out_ref.dtype)
        else:
            out_ref[0] = total


def add_piece(sky, wigner, beam, meta, before, final):
    slots, piece_rows, columns = sky.shape
    _, k_local, cycles, _ = wigner.shape
    rows = k_local * cycles
    tile = tile_of(piece_rows)
    tiles = piece_rows // tile

    def at(slot, step, meta):
        return jnp.minimum(jnp.maximum(step, meta[4 + slot]), tiles - 1)

    in_specs = [
        pl.BlockSpec((1, tile, columns), lambda s, t, meta: (s, at(s, t, meta), 0)),
        pl.BlockSpec((1, k_local, cycles, tile), lambda s, t, meta: (s, 0, 0, meta[6] + at(s, t, meta))),
        pl.BlockSpec((k_local, 2, tile), lambda s, t, meta: (0, 0, meta[6] + at(s, t, meta))),
    ]
    operands = [sky, wigner, beam]
    block = pl.BlockSpec((1, rows, columns), lambda s, t, meta: (s, 0, 0))
    if before is not None:
        in_specs.append(block)
        operands.append(before)
    scratch = [
        pltpu.VMEM((2 * rows, tile), jnp.bfloat16),
        pltpu.VMEM((2 * rows, columns), jnp.float32),
    ]
    if final:
        scratch.append(pltpu.VMEM((columns // 128, rows, 128), jnp.float32))
    return pl.pallas_call(
        functools.partial(kernel, tile, tiles, before is None, final),
        out_shape=jax.ShapeDtypeStruct((slots, rows, columns), jnp.bfloat16 if final else jnp.float32),
        grid_spec=pltpu.PrefetchScalarGridSpec(
            num_scalar_prefetch=1,
            grid=(slots, tiles),
            in_specs=in_specs,
            out_specs=block,
            scratch_shapes=scratch,
        ),
        compiler_params=pltpu.CompilerParams(vmem_limit_bytes=24 * 1024 * 1024),
        cost_estimate=pl.CostEstimate(
            flops=2 * slots * 2 * rows * piece_rows * columns // 2,
            bytes_accessed=2 * slots * (rows + columns) * piece_rows // 2,
            transcendentals=0,
        ),
        name="convolve_last" if final else "convolve",
    )(meta, *operands)


def local(sky, beam, wigner, m_list, *, ways):
    slots, piece_rows, columns = sky.shape
    k_local, cycles = wigner.shape[1], wigner.shape[2]
    tile = tile_of(piece_rows)
    tiles = piece_rows // tile
    me = lax.axis_index("beamk")
    first_k = me * k_local - KB // 2

    def meta_of(owner):
        first_tile = jnp.clip((m_list - owner * piece_rows) // tile, 0, tiles)
        return jnp.concatenate(
            [
                jnp.stack([owner * piece_rows, first_k]),
                m_list,
                first_tile,
                (owner * tiles)[None],
            ]
        ).astype(jnp.int32)

    pieces = [sky]
    for shift in range(1, ways):
        perm = [(c, (c + shift) % ways) for c in range(ways)]
        pieces.append(lax.ppermute(sky, "beamk", perm))
    total = None
    for shift, piece in enumerate(pieces):
        owner = lax.rem(me - shift + ways, ways)
        total = add_piece(piece, wigner, beam, meta_of(owner), total, shift == ways - 1)
    parts = total.reshape(slots, cycles, k_local, columns).transpose(1, 0, 2, 3)
    parts = parts.reshape(cycles, slots * k_local, columns)
    received = lax.all_to_all(parts, "blk", split_axis=0, concat_axis=0, tiled=True)
    return received.reshape(1, -1, k_local, columns)


def solution(mesh):
    in_specs = (
        P("blk", "beamk", None),
        P("beamk", None, None),
        P("blk", "beamk", None, None),
        P("blk"),
    )
    out_specs = P("blk", None, "beamk", None)
    body = functools.partial(local, ways=mesh.shape["beamk"])
    return jax.shard_map(body, mesh=mesh, in_specs=in_specs, out_specs=out_specs, check_vma=False)
```

time: 181 us -> 38.9 us (0.21)
  matrix products: 84.2 us -> 0 us
  other arithmetic: 37.4 us -> 0.67 us
  waiting for transfers between devices: 16.2 us -> 0.01 us
  between operations: 13.6 us -> 0.07 us
  Pallas kernels: 0 us -> 6.96 us
    dot_general x12 -> x0, matrix products: 84.2 us -> none  [slot_term(): jnp.einsum('krl,kls->rks', wigner_rows, product, preferred_element_type=j...]
    sub x6 -> x0, other arithmetic: 34.3 us -> none  [slot_term(): sky_re[None] * beam_re[:, :, None] - sky_im[None] * beam_im[:, :, None]]
    all_gather x1 -> x0, waiting for transfers between devices: 15.5 us -> none  [local(): sky_piece = lax.all_gather(sky, 'beamk', axis=1, tiled=True)]
    pallas_call x0 -> x2, Pallas kernels: none -> 6.96 us  [add_piece(): pl.pallas_call(functools.partial(kernel, tile, tiles, before is None, fin...]
    unnamed x6 -> x8, local copies, waits for them, and re-layouts: 0.01 us -> 4.82 us
    squeeze x2 -> x0, local copies, waits for them, and re-layouts: 2.9 us -> none  [the longest x1 2.81 us: with_term(): sky_block[slot]]
  transfers between devices with their start and end apart: 1 -> 1, of which waited for: 1 -> 0; matrix products, arithmetic and copies ran while one was open for 2% -> 6% of each run, Pallas kernels for 0% -> 8%
where the time goes in v1:
time: 38.9 us; the launch traced here: 38.6 us
  blocking collectives  22.5 us (58%)
  local copies, waits for them, and re-layouts  7.89 us (20%)
  Pallas kernels  6.96 us (18%)
  other arithmetic  0.67 us (2%)
  starting transfers between devices  0.45 us (1%)
    all_to_all x1, blocking collectives, local(): lax.all_to_all(parts, 'blk', split_axis=0, concat_axis=0, tiled=True)  22.5 us
    pallas_call x2, Pallas kernels, add_piece(): pl.pallas_call(functools.partial(kernel, tile, tiles, before is None, fin...  6.96 us
    unnamed x8, local copies, waits for them, and re-layouts  4.82 us
    concatenate x2, local copies, waits for them, and re-layouts, meta_of(): jnp.concatenate([jnp.stack([owner * piece_rows, first_k]), m_list, first_...  1.47 us
    reshape x2, local copies, waits for them, and re-layouts, local(): return received.reshape(1, -1, k_local, columns)  0.94 us
  transfers between devices with their start and end apart: 1, of which 0 were waited for; matrix products, arithmetic and copies ran while one was open for 6% of the time, Pallas kernels for 8%

profile of v1, /device:TPU:0, one launch (start us, length us, event | category | flops | bytes accessed | tf_op | source)
XLA Modules:
  0.0 38.6 jit_solution(8810800394865584302)
XLA Ops:
  0.0 0.5 %collective-permute-start = (bf16[2,1536,384]{2,1,0:T(8,128)(2,1)}, bf16[2,1536,384]{2,1,0:T(8,128)(2,1)S(1)}, u32[]{:S(2)}, u32[]{:S(2)}) collective-permute-start(bf16[2,1536,384]{2,1,0:T(8,128)(2,1)} %refs_0_.1), channel_id=1, source_target_pairs={{0,1},{1,0},{2,3},{3,2},{4,5},{5,4},{6,7},{7,6},{8,9},{9,8},{10,11... | collective-permute-start | bytes 7077896 | tf_op jit(solution)/shard_map/ppermute | solution.py:142
  0.5 0.7 %fusion = (s32[2]{0:T(128)S(1)}, s32[2]{0:T(128)S(1)}) fusion(s32[2]{0:T(128)} %param.7, s32[]{:T(128)} %mul.20, s32[]{:T(128)} %mul.17), kind=kLoop, calls=%fused_computation.8 | loop fusion | flops 68 | bytes 32 | tf_op jit(solution)/shard_map/jit(clip)/min | solution.py:129
  1.1 0.7 %concatenate.6.meta = s32[7]{0:T(128)S(1)} concatenate(s32[1]{0:T(128)} %bitcast, s32[1]{0:T(128)} %bitcast.1, s32[2]{0:T(128)} %param.7, s32[2]{0:T(128)S(1)} %get-tuple-element.6, s32[1]{0:T(128)} %bitcast.2), dimensions={0} | concatenate | bytes 56 | tf_op jit(solution)/shard_map/concatenate | solution.py:130
  1.9 0.7 %concatenate.7.meta = s32[7]{0:T(128)S(1)} concatenate(s32[1]{0:T(128)} %bitcast.3, s32[1]{0:T(128)} %bitcast.1, s32[2]{0:T(128)} %param.7, s32[2]{0:T(128)S(1)} %get-tuple-element.5, s32[1]{0:T(128)} %bitcast.4), dimensions={0} | concatenate | bytes 56 | tf_op jit(solution)/shard_map/concatenate | solution.py:130
  2.6 0.0 copy-start
  2.6 2.1 %copy-done = bf16[2,20,16,3072]{3,2,1,0:T(8,128)(2,1)S(1)} copy-done((bf16[2,20,16,3072]{3,2,1,0:T(8,128)(2,1)S(1)}, bf16[2,20,16,3072]{3,2,1,0:T(8,128)(2,1)}, u32[]{:S(2)}) %copy-start) | copy-done | bytes 3932184
  4.7 0.0 copy-start.2
  4.7 1.7 %copy-done.2 = bf16[2,1536,384]{2,1,0:T(8,128)(2,1)S(1)} copy-done((bf16[2,1536,384]{2,1,0:T(8,128)(2,1)S(1)}, bf16[2,1536,384]{2,1,0:T(8,128)(2,1)}, u32[]{:S(2)}) %copy-start.2) | copy-done | bytes 2359320
  6.4 0.0 copy-start.3
  6.4 1.0 %copy-done.3 = f32[20,2,3072]{2,1,0:T(2,128)S(1)} copy-done((f32[20,2,3072]{2,1,0:T(2,128)S(1)}, f32[20,2,3072]{2,1,0:T(2,128)}, u32[]{:S(2)}) %copy-start.3) | copy-done | bytes 491544
  7.4 0.0 copy-start.1
  7.4 3.2 %convolve.1.refs_3_ = f32[2,320,384]{2,1,0:T(8,128)S(1)} custom-call(s32[7]{0:T(128)S(1)} %concatenate.7.meta, bf16[2,1536,384]{2,1,0:T(8,128)(2,1)S(1)} %copy-done.2, bf16[2,20,16,3072]{3,2,1,0:T(8,128)(2,1)S(1)} %copy-done, f32[20,2,3072]{2,1,0:T(2,128)S(1)} %copy-done.3), custom_call_target="tpu_custom_call" | custom-call | flops 754974720 | bytes 2162688 | tf_op jit(solution)/shard_map/convolve/pallas_call | solution.py:100
  10.6 0.0 collective-permute-done.refs_0_
  10.6 0.0 copy-done.1
  10.6 3.8 %convolve_last.1 = bf16[2,320,384]{2,1,0:T(8,128)(2,1)S(1)} custom-call(s32[7]{0:T(128)S(1)} %concatenate.6.meta, bf16[2,1536,384]{2,1,0:T(8,128)(2,1)S(1)} %collective-permute-done.refs_0_, bf16[2,20,16,3072]{3,2,1,0:T(8,128)(2,1)S(1)} %copy-done.1, f32[20,2,3072]{2,1,0:T(2,128)S(1)} %copy-done.3, f32[2,320,384]{2,1,0:T(8,128)S(1)} %convolve.1.refs_3_), custom_call_target="tpu_custom_call" | custom-call | flops 754974720 | bytes 2162688 | tf_op jit(solution)/shard_map/convolve_last/pallas_call | solution.py:100
  14.4 0.5 %copy.9 = bf16[2,320,384]{2,0,1:T(2,128)(2,1)S(1)} copy(bf16[2,320,384]{2,1,0:T(8,128)(2,1)S(1)} %convolve_last.1) | data formatting | bytes 983040 | tf_op jit(solution)/shard_map/convolve_last/pallas_call | solution.py:100
  14.9 0.1 copy.10
  15.0 0.1 copy.11
  15.1 22.5 %all_to_all.5 = bf16[16,40,384]{2,1,0:T(8,128)(2,1)S(1)} all-to-all(bf16[16,40,384]{2,1,0:T(8,128)(2,1)S(1)} %copy.11), channel_id=1, replica_groups=mesh['blk'=16,'beamk'=2] {'blk'}, dimensions={0} | all-to-all | bytes 983040 | tf_op jit(solution)/shard_map/all_to_all | solution.py:149
  37.6 0.1 reshape.11
  37.7 0.8 %copy.12 = bf16[1,32,20,384]{3,1,2,0:T(8,128)(2,1)} copy(bf16[1,32,20,384]{3,2,1,0:T(8,128)(2,1)S(1)} %reshape.11) | data formatting | bytes 983040 | tf_op jit(solution)/shard_map/reshape | solution.py:150
Async XLA Ops:
  0.0 10.6 %collective-permute-start = (bf16[2,1536,384]{2,1,0:T(8,128)(2,1)}, bf16[2,1536,384]{2,1,0:T(8,128)(2,1)S(1)}, u32[]{:S(2)}, u32[]{:S(2)}) collective-permute-start(bf16[2,1536,384]{2,1,0:T(8,128)(2,1)} %refs_0_.1), channel_id=1, source_target_pairs={{0,1},{1,0},{2,3},{3,2},{4,5},{5,4},{6,7},{7,6},{8,9},{9,8},{10,11... | collective-permute-start | bytes 7077896 | tf_op jit(solution)/shard_map/ppermute | solution.py:142
  2.6 2.1 %copy-start = (bf16[2,20,16,3072]{3,2,1,0:T(8,128)(2,1)S(1)}, bf16[2,20,16,3072]{3,2,1,0:T(8,128)(2,1)}, u32[]{:S(2)}) copy-start(bf16[2,20,16,3072]{3,2,1,0:T(8,128)(2,1)} %refs_1_.3) | copy-start | bytes 11796484
  4.7 1.7 %copy-start.2 = (bf16[2,1536,384]{2,1,0:T(8,128)(2,1)S(1)}, bf16[2,1536,384]{2,1,0:T(8,128)(2,1)}, u32[]{:S(2)}) copy-start(bf16[2,1536,384]{2,1,0:T(8,128)(2,1)} %refs_0_.1) | copy-start | bytes 7077892
  6.4 1.0 %copy-start.3 = (f32[20,2,3072]{2,1,0:T(2,128)S(1)}, f32[20,2,3072]{2,1,0:T(2,128)}, u32[]{:S(2)}) copy-start(f32[20,2,3072]{2,1,0:T(2,128)} %refs_2_.3) | copy-start | bytes 1474564
  7.4 3.2 %copy-start.1 = (bf16[2,20,16,3072]{3,2,1,0:T(8,128)(2,1)S(1)}, bf16[2,20,16,3072]{3,2,1,0:T(8,128)(2,1)}, u32[]{:S(2)}) copy-start(bf16[2,20,16,3072]{3,2,1,0:T(8,128)(2,1)} %refs_1_.3) | copy-start | bytes 11796484
